TPU v7x, 32 devices: a whole 2x2x4 slice. The times are simulated.
32 devices in a mesh: group: 2 (over x), route: 4 (over y, core), cuts: 4 (over z).
Axes of the slice: x: 2, y: 2, z: 4, core: 2. Of those that a mesh axis runs over, the one named last changes fastest.
Arguments:
- query_matrix_rows: bfloat16 [1024, 4096], P(('group', 'route'), 'cuts'), parts along dimension 0, may hold values from -8 to 8
- key_matrix_rows: bfloat16 [1024, 1024], P(('group', 'route'), 'cuts'), parts along dimension 0, may hold values from -8 to 8
- value_matrix_rows: bfloat16 [1024, 1024], P(('group', 'route'), 'cuts'), parts along dimension 0, may hold values from -6 to 6
- attention_output_matrix: bfloat16 [4096, 4096], P('cuts'), may hold values from -0.125 to 0.125
- residual: bfloat16 [1024, 4096], P(('group', 'route'), 'cuts'), parts along dimension 0, may hold values from -6 to 6
- cotangent: bfloat16 [1024, 4096], P(('group', 'route'), 'cuts'), parts along dimension 0, may hold values from -0.59765625 to 0.59765625
- token_expert_choices: int32 [1024, 2], P(('group', 'route')), parts along dimension 0, may hold values from 0 to 3, as said below
- token_slot_positions: int32 [1024, 2], P(('group', 'route')), parts along dimension 0, may hold values from 0 to 127, as said below
- router_choice_weight: float32 [1024, 2], P(('group', 'route')), parts along dimension 0, may hold values from 0.2 to 1
- expert_gate_weight: bfloat16 [4, 3200, 4096], P('route', 'cuts'), may hold values from -0.09375 to 0.09375
- expert_down_weight: bfloat16 [4, 3200, 4096], P('route', 'cuts'), may hold values from -0.15625 to 0.15625
- adapter_down_factor: bfloat16 [4, 64, 4096], P('route'), may hold values from -0.09375 to 0.09375
- adapter_up_factor: bfloat16 [4, 64, 3200], P('route', None, 'cuts'), may hold values from -0.75 to 0.75
Outputs:
- layer_out: bfloat16 [1024, 4096], P(('group', 'route'), 'cuts'), parts along dimension 0
- down_factor_gradient: float32 [8, 64, 4096], P(('group', 'route'), None, 'cuts'), parts along dimension 0
- up_factor_gradient: float32 [8, 64, 3200], P(('group', 'route'), None, 'cuts'), parts along dimension 0
There are 2 independent parts, one for each index of `group`. A program takes and returns all parts, laid end to end along the dimension named above; an argument that names none is the same for every part. Nothing has to cross between parts.
Inputs may be any that keep to these rules, and one draw needn't show every extreme that they name: `token_expert_choices`: the two experts of a token differ. Within one sequence of 128 tokens no expert is named more than 128 times; one expert, the same for all sequences of a draw, is named exactly 128 times in every sequence. `token_slot_positions`: within one sequence the slots given for one expert are all different.
All inputs are finite; a program needn't handle non-finite values.
Results may differ from a plain program's by a relative error of at most 0.014.
Values may be sent and summed in bfloat16 or wider, within the bound.
A program may use at most 128 MiB of HBM per device.

v0:
```python
import math

import jax
import jax.numpy as jnp
from jax import lax
from jax.sharding import PartitionSpec as P

HEAD_DIM = 128


ADAPTER_SCALE = 0.5


def causal_heads(query_matrix_rows, key_matrix_rows, value_matrix_rows):
    length = query_matrix_rows.shape[0]
    kv_local = key_matrix_rows.shape[1] // HEAD_DIM
    per_kv = query_matrix_rows.shape[1] // key_matrix_rows.shape[1]
    queries = query_matrix_rows.reshape(length, kv_local, per_kv, HEAD_DIM)
    key_view = key_matrix_rows.reshape(length, kv_local, HEAD_DIM)
    value_view = value_matrix_rows.reshape(length, kv_local, HEAD_DIM)
    scores = jnp.einsum(
        "qhgd,khd->hgqk", queries, key_view, preferred_element_type=jnp.float32
    ) / math.sqrt(HEAD_DIM)
    future = lax.broadcasted_iota(jnp.int32, (length, length), 1) > lax.broadcasted_iota(
        jnp.int32, (length, length), 0
    )
    scores = jnp.where(future, -jnp.inf, scores)
    row_max = jnp.max(scores, axis=-1, keepdims=True)
    shifted = jnp.exp(scores - row_max)
    weights = (shifted / jnp.sum(shifted, axis=-1, keepdims=True)).astype(jnp.bfloat16)
    attended = jnp.einsum("hgqk,khd->qhgd", weights, value_view, preferred_element_type=jnp.float32)
    return attended.astype(jnp.bfloat16).reshape(length, query_matrix_rows.shape[1])


def fill_slots(source_rows, owners):
    padded = jnp.concatenate(
        [source_rows, jnp.zeros((1, source_rows.shape[1]), source_rows.dtype)], axis=0
    )
    return jnp.take(padded, owners, axis=0)


def weighted_slots(source_rows, owners, scales):
    return (fill_slots(source_rows, owners).astype(jnp.float32) * scales[:, None]).astype(
        jnp.bfloat16
    )


def combine_rows(returned, cell_ids, router_choice_weight):
    first_out = jnp.take(returned, cell_ids[:, 0], axis=0)
    second_out = jnp.take(returned, cell_ids[:, 1], axis=0)
    return router_choice_weight[:, 0:1] * first_out + router_choice_weight[:, 1:2] * second_out


def local(
    query_matrix_rows,
    key_matrix_rows,
    value_matrix_rows,
    attention_output_matrix,
    residual,
    cotangent,
    token_expert_choices,
    token_slot_positions,
    router_choice_weight,
    expert_gate_weight,
    expert_down_weight,
    adapter_down_factor,
    adapter_up_factor,
):
    attended = causal_heads(query_matrix_rows, key_matrix_rows, value_matrix_rows)
    head_terms = jnp.dot(attended, attention_output_matrix, preferred_element_type=jnp.float32)
    head_cols = lax.psum_scatter(head_terms, "cuts", scatter_dimension=1, tiled=True)
    hidden_cols = (residual.astype(jnp.float32) + head_cols).astype(jnp.bfloat16)
    length = residual.shape[0]
    col_count = residual.shape[1]
    model_width = expert_gate_weight.shape[2]
    experts = lax.axis_size("route")
    capacity = 4 * length // experts
    cell_ids = token_expert_choices * capacity + token_slot_positions
    flat_cells = cell_ids.reshape(-1)
    owners = (
        jnp.full((experts * capacity,), length, jnp.int32)
        .at[flat_cells]
        .set(jnp.repeat(jnp.arange(length, dtype=jnp.int32), 2))
    )
    scales = (
        jnp.zeros((experts * capacity,), jnp.float32)
        .at[flat_cells]
        .set(router_choice_weight.reshape(-1))
    )
    full_x, full_g = (
        lax.all_gather(hidden_cols, "cuts", axis=1, tiled=True),
        lax.all_gather(cotangent, "cuts", axis=1, tiled=True),
    )
    token_part = fill_slots(full_x, owners).reshape(experts, capacity, model_width)
    grad_part = weighted_slots(full_g, owners, scales).reshape(experts, capacity, model_width)
    slot_x, slot_g = (
        lax.all_to_all(token_part, "route", split_axis=0, concat_axis=0, tiled=True),
        lax.all_to_all(grad_part, "route", split_axis=0, concat_axis=0, tiled=True),
    )
    expert_input_rows = slot_x.reshape(-1, model_width)
    rows_g = slot_g.reshape(-1, model_width)
    reduce_final_axis = (((1,), (1,)), ((), ()))
    contract_first = (((0,), (0,)), ((), ()))
    gate_primary_product = lax.dot_general(
        expert_input_rows,
        expert_gate_weight[0],
        reduce_final_axis,
        preferred_element_type=jnp.float32,
    )
    adapter_product = lax.dot_general(
        expert_input_rows,
        adapter_down_factor[0],
        reduce_final_axis,
        preferred_element_type=jnp.float32,
    ).astype(jnp.bfloat16)
    gate_preactivation = gate_primary_product + ADAPTER_SCALE * jnp.dot(
        adapter_product, adapter_up_factor[0], preferred_element_type=jnp.float32
    )
    sigmoid_gate = jax.nn.sigmoid(gate_preactivation)
    activ = (gate_preactivation * sigmoid_gate).astype(jnp.bfloat16)
    partial_out = jnp.dot(activ, expert_down_weight[0], preferred_element_type=jnp.float32).astype(
        jnp.bfloat16
    )
    slot_sums = lax.psum_scatter(
        partial_out.astype(jnp.float32)
        .reshape(experts, capacity, model_width)
        .astype(jnp.bfloat16),
        "cuts",
        scatter_dimension=2,
        tiled=True,
    ).astype(jnp.float32)
    returned = (
        lax.all_to_all(
            slot_sums.astype(jnp.bfloat16), "route", split_axis=0, concat_axis=0, tiled=True
        )
        .astype(slot_sums.dtype)
        .reshape(experts * capacity, col_count)
    )
    merged = hidden_cols.astype(jnp.float32) + combine_rows(
        returned, cell_ids, router_choice_weight
    )
    layer_out = merged.astype(jnp.bfloat16)
    grad_hidden = lax.dot_general(
        rows_g, expert_down_weight[0], reduce_final_axis, preferred_element_type=jnp.float32
    )
    preactivation_gradient = (
        grad_hidden * sigmoid_gate * (1.0 + gate_preactivation * (1.0 - sigmoid_gate))
    ).astype(jnp.bfloat16)
    up_factor_gradient = ADAPTER_SCALE * lax.dot_general(
        adapter_product, preactivation_gradient, contract_first, preferred_element_type=jnp.float32
    )
    factor_part = lax.dot_general(
        preactivation_gradient,
        adapter_up_factor[0],
        reduce_final_axis,
        preferred_element_type=jnp.float32,
    ).astype(jnp.bfloat16)
    gradient_pieces = lax.dot_general(
        factor_part, expert_input_rows, contract_first, preferred_element_type=jnp.float32
    )
    down_factor_gradient = ADAPTER_SCALE * lax.psum_scatter(
        gradient_pieces.astype(jnp.bfloat16), "cuts", scatter_dimension=1, tiled=True
    ).astype(jnp.float32)
    return (layer_out, down_factor_gradient[None], up_factor_gradient[None])


def solution(mesh):
    return jax.shard_map(
        local,
        mesh=mesh,
        in_specs=(
            P(("group", "route"), "cuts"),
            P(("group", "route"), "cuts"),
            P(("group", "route"), "cuts"),
            P("cuts", None),
            P(("group", "route"), "cuts"),
            P(("group", "route"), "cuts"),
            P(("group", "route"), None),
            P(("group", "route"), None),
            P(("group", "route"), None),
            P("route", "cuts", None),
            P("route", "cuts", None),
            P("route", None, None),
            P("route", None, "cuts"),
        ),
        out_specs=(
            P(("group", "route"), "cuts"),
            P(("group", "route"), None, "cuts"),
            P(("group", "route"), None, "cuts"),
        ),
        check_vma=False,
    )
```

profile of v0, /device:TPU:0, one launch (start us, length us, event | category | flops | bytes accessed | tf_op | source)
XLA Modules:
  0.0 290.7 jit_solution(17472282540791643243)
XLA Ops:
  11.2 6.0 %fusion.44 = f32[128,4096]{1,0:T(8,128)} fusion(bf16[128,1024]{0,1:T(8,128)(2,1)S(1)} %bitcast.77, bf16[1024,4096]{1,0:T(8,128)(2,1)} %param.20), kind=kOutput, calls=%fused_computation.69 | convolution fusion | flops 1073741824 | bytes 10747904 | tf_op jit(solution)/shard_map/dot_general | solution.py:70
  17.3 46.7 %reduce-scatter.4.cloned.1.call-done = f32[128,1024]{1,0:T(8,128)} async-done(((f32[128,4096]{1,0:T(8,128)}), f32[128,1024]{1,0:T(8,128)}) %reduce-scatter.4.cloned.1.call-update) | async-done | bytes 524304 | tf_op jit(solution)/shard_map/reduce_scatter | solution.py:71
  63.9 1.8 add_convert_fusion
  67.7 25.8 %all-gather.3.cloned.1.call-done = bf16[128,4096]{1,0:T(8,128)(2,1)} async-done(((bf16[128,1024]{1,0:T(8,128)(2,1)}), bf16[128,4096]{1,0:T(8,128)(2,1)}) %all-gather.3.cloned.1.call-update) | async-done | bytes 1048592 | tf_op jit(solution)/shard_map/all_gather | solution.py:91
  94.8 4.4 %gather_fusion = bf16[512,4096]{1,0:T(8,128)(2,1)} fusion(bf16[129,4096]{1,0:T(8,128)(2,1)S(1)} %concatenate.6, s32[1024]{0:T(1024)S(1)} %pad_clamp_fusion.2), kind=kCustom, calls=%fused_computation.clone | custom fusion | bytes 8390656 | tf_op jit(solution)/shard_map/jit(_take)/gather | solution.py:39
  99.2 4.6 %broadcast_select_fusion = bf16[512,4096]{1,0:T(8,128)(2,1)} fusion(bf16[512,4096]{1,0:T(8,128)(2,1)} %gather_fusion, pred[512]{0:T(512)(128)(4,1)S(1)} %compare_and_fusion.2), kind=kLoop, calls=%fused_computation.16 | loop fusion | flops 2097152 | bytes 8389120 | tf_op jit(solution)/shard_map/jit(_take)/select_n | solution.py:39
  103.8 4.8 %all-to-all-start = ((bf16[4,128,4096]{2,1,0:T(8,128)(2,1)}), bf16[4,128,4096]{2,1,0:T(8,128)(2,1)}, u32[]{:S(2)}, u32[]{:S(2)}) async-start(bf16[4,128,4096]{2,1,0:T(8,128)(2,1)} %bitcast.74), calls=%async_computation.1 | async-start | bytes 8388608 | tf_op jit(solution)/shard_map/all_to_all | solution.py:97
  109.4 47.4 %all-to-all-done = bf16[4,128,4096]{2,1,0:T(8,128)(2,1)} async-done(((bf16[4,128,4096]{2,1,0:T(8,128)(2,1)}), bf16[4,128,4096]{2,1,0:T(8,128)(2,1)}, u32[]{:S(2)}, u32[]{:S(2)}) %all-to-all-start) | async-done | bytes 4194336 | tf_op jit(solution)/shard_map/all_to_all | solution.py:97
  156.8 7.0 %fusion.5 = f32[512,800]{0,1:T(8,128)S(1)} fusion(bf16[512,4096]{1,0:T(8,128)(2,1)} %bitcast.11, bf16[1,800,4096]{2,1,0:T(8,128)(2,1)} %param.26), kind=kOutput, calls=%fused_computation.12 | convolution fusion | flops 3355443200 | bytes 12386304 | tf_op jit(solution)/shard_map/dot_general | solution.py:104
  163.9 3.6 %convolution_convert_fusion.3 = bf16[512,64]{0,1:T(8,128)(2,1)S(1)} fusion(bf16[512,4096]{1,0:T(8,128)(2,1)} %bitcast.11, bf16[1,64,4096]{2,1,0:T(8,128)(2,1)S(1)} %copy-done), kind=kOutput, calls=%fused_computation.30 | convolution fusion | flops 268468224 | bytes 4784128 | tf_op jit(solution)/shard_map/dot_general | solution.py:110
  167.9 9.1 %fusion.7 = bf16[512,4096]{1,0:T(8,128)(2,1)} fusion(bf16[1,800,4096]{2,1,0:T(8,128)(2,1)} %param.27, f32[512,800]{0,1:T(8,128)S(1)} %multiply_add_fusion), kind=kOutput, calls=%fused_computation.14 | convolution fusion | flops 3359588352 | bytes 12386304 | tf_op jit(solution)/shard_map/dot_general | solution.py:121
  178.0 1.4 scatter_custom_fusion.1
  180.7 4.4 %gather_fusion.3 = bf16[512,4096]{1,0:T(8,128)(2,1)} fusion(bf16[129,4096]{1,0:T(8,128)(2,1)S(1)} %concatenate.7, s32[1024]{0:T(1024)S(1)} %pad_clamp_fusion.2), kind=kCustom, calls=%fused_computation.2.clone | custom fusion | bytes 8390656 | tf_op jit(solution)/shard_map/jit(_take)/gather | solution.py:39
  185.1 4.7 %multiply_convert_fusion = bf16[512,4096]{1,0:T(8,128)(2,1)S(1)} fusion(bf16[512,4096]{1,0:T(8,128)(2,1)} %gather_fusion.3, f32[512]{0:T(512)S(1)} %scatter_custom_fusion.1, pred[512]{0:T(512)(128)(4,1)S(1)} %compare_and_fusion.2), kind=kLoop, calls=%fused_computation.7 | loop fusion | flops 8388608 | bytes 8391168 | tf_op jit(solution)/shard_map/convert_element_type | solution.py:43
  189.9 50.9 %all_to_all.15 = bf16[4,128,4096]{2,1,0:T(8,128)(2,1)S(1)} all-to-all(bf16[4,128,4096]{2,1,0:T(8,128)(2,1)S(1)} %bitcast.73), channel_id=1, replica_groups=mesh['group'=2,'route'=4,'cuts'=4] {'route'}, dimensions={0} | all-to-all | bytes 8388608 | tf_op jit(solution)/shard_map/all_to_all | solution.py:98
  240.7 3.9 %multiply_convert_fusion.1 = bf16[512,800]{0,1:T(8,128)(2,1)S(1)} fusion(f32[512,800]{0,1:T(8,128)S(1)} %multiply_add_fusion, bf16[512,4096]{1,0:T(8,128)(2,1)S(1)} %bitcast.76, bf16[1,800,4096]{2,1,0:T(8,128)(2,1)S(1)} %bitcast.84), kind=kOutput, calls=%fused_computation.17 | convolution fusion | flops 3359129600 | bytes 13205504 | tf_op jit(solution)/shard_map/dot_general | solution.py:143
  244.7 4.6 %convolution_convert_fusion = bf16[64,4096]{1,0:T(8,128)(2,1)} fusion(bf16[512,4096]{1,0:T(8,128)(2,1)} %bitcast.11, bf16[512,800]{0,1:T(8,128)(2,1)S(1)} %multiply_convert_fusion.1, bf16[1,64,800]{2,1,0:T(8,128)(2,1)S(1)} %copy-done.3), kind=kOutput, calls=%fused_computation.15 | convolution fusion | flops 321159168 | bytes 5640192 | tf_op jit(solution)/shard_map/dot_general | solution.py:158
  249.3 3.3 %reduce-scatter.6.cloned.1.call-done = bf16[4,128,1024]{2,1,0:T(8,128)(2,1)} async-done(((bf16[4,128,4096]{2,1,0:T(8,128)(2,1)}), bf16[4,128,1024]{2,1,0:T(8,128)(2,1)}) %reduce-scatter.6.cloned.1.call-update) | async-done | bytes 1048592 | tf_op jit(solution)/shard_map/reduce_scatter | solution.py:124
  252.6 4.2 %all-to-all-start.1 = ((bf16[4,128,1024]{2,1,0:T(8,128)(2,1)}), bf16[4,128,1024]{2,1,0:T(8,128)(2,1)}, u32[]{:S(2)}, u32[]{:S(2)}) async-start(bf16[4,128,1024]{2,1,0:T(8,128)(2,1)} %reduce-scatter.6.cloned.1.call-done), calls=%async_computation.3 | async-start | bytes 2097152 | tf_op jit(solution)/shard_map/all_to_all | solution.py:133
  257.9 18.7 %reduce-scatter.8.cloned.1.call-done = bf16[64,1024]{1,0:T(8,128)(2,1)} async-done(((bf16[64,4096]{1,0:T(8,128)(2,1)}), bf16[64,1024]{1,0:T(8,128)(2,1)}) %reduce-scatter.8.cloned.1.call-update) | async-done | bytes 131088 | tf_op jit(solution)/shard_map/reduce_scatter | solution.py:161
  276.7 1.6 multiply_bitcast_fusion
  278.3 1.5 bitcast_convert_fusion
  280.6 1.6 gather_fusion.2
  282.2 2.0 fusion.21
  (60 shorter events, 12.5 us)
Async XLA Ops:
  7.2 156.7 %copy-start = (bf16[1,64,4096]{2,1,0:T(8,128)(2,1)S(1)}, bf16[1,64,4096]{2,1,0:T(8,128)(2,1)}, u32[]{:S(2)}) copy-start(bf16[1,64,4096]{2,1,0:T(8,128)(2,1)} %param.28) | copy-start | bytes 1572868
  7.2 56.8 %reduce-scatter.4.cloned.1.call-start = ((), (), s32[]{:S(2)}) async-start(), calls=%async_computation.6 | async-start | bytes 2621440 | tf_op jit(solution)/shard_map/reduce_scatter | solution.py:71
  11.1 52.8 %copy-start.4 = (bf16[128,1024]{1,0:T(8,128)(2,1)S(1)}, bf16[128,1024]{1,0:T(8,128)(2,1)}, u32[]{:S(2)}) copy-start(bf16[128,1024]{1,0:T(8,128)(2,1)} %param.21) | copy-start | bytes 786436
  11.1 54.6 %copy-start.6 = (s32[128,2]{0,1:T(2,128)S(1)}, s32[128,2]{0,1:T(2,128)}, u32[]{:S(2)}) copy-start(s32[128,2]{0,1:T(2,128)} %param.24) | copy-start | bytes 3076
  11.1 54.6 %copy-start.7 = (s32[128,2]{0,1:T(2,128)S(1)}, s32[128,2]{0,1:T(2,128)}, u32[]{:S(2)}) copy-start(s32[128,2]{0,1:T(2,128)} %param.23) | copy-start | bytes 3076
  17.2 76.2 %all-gather.3.cloned.1.call-start = ((), (), s32[]{:S(2)}) async-start(), calls=%async_computation.7 | async-start | bytes 1310720 | tf_op jit(solution)/shard_map/all_gather | solution.py:91
  103.8 53.1 %all-to-all-start = ((bf16[4,128,4096]{2,1,0:T(8,128)(2,1)}), bf16[4,128,4096]{2,1,0:T(8,128)(2,1)}, u32[]{:S(2)}, u32[]{:S(2)}) async-start(bf16[4,128,4096]{2,1,0:T(8,128)(2,1)} %bitcast.74), calls=%async_computation.1 | async-start | bytes 8388608 | tf_op jit(solution)/shard_map/all_to_all | solution.py:97
  108.6 70.8 %all-gather.5.cloned.1.call-start = ((), (), s32[]{:S(2)}) async-start(), calls=%async_computation.9 | async-start | bytes 1310720 | tf_op jit(solution)/shard_map/all_gather | solution.py:92
  109.4 143.2 %reduce-scatter.6.cloned.1.call-start = ((), (), s32[]{:S(2)}) async-start(), calls=%async_computation.8 | async-start | bytes 5242880 | tf_op jit(solution)/shard_map/reduce_scatter | solution.py:124
  163.9 3.6 %copy-start.3 = (bf16[1,64,800]{2,1,0:T(8,128)(2,1)S(1)}, bf16[1,64,800]{2,1,0:T(8,128)(2,1)}, u32[]{:S(2)}) copy-start(bf16[1,64,800]{2,1,0:T(8,128)(2,1)} %param.29) | copy-start | bytes 307204
  177.0 0.7 copy-start.5
  177.1 99.6 %reduce-scatter.8.cloned.1.call-start = ((), (), s32[]{:S(2)}) async-start(), calls=%async_computation.10 | async-start | bytes 655360 | tf_op jit(solution)/shard_map/reduce_scatter | solution.py:161
  185.1 55.6 %slice-start = ((s8[6553600]{0:T(1024)(128)(4,1)}), s8[4194304]{0:T(1024)(128)(4,1)S(1)}, s32[]{:S(2)}) async-start(s8[6553600]{0:T(1024)(128)(4,1)} %bitcast.83), calls=%async_computation.11 | async-start | bytes 8388608
  189.9 50.9 %slice-start.1 = ((s8[6553600]{0:T(1024)(128)(4,1)}), s8[2359296]{0:T(1024)(128)(4,1)S(1)}, s32[]{:S(2)}) async-start(s8[6553600]{0:T(1024)(128)(4,1)} %bitcast.83), calls=%async_computation.12 | async-start | bytes 4718592
  252.6 25.7 %all-to-all-start.1 = ((bf16[4,128,1024]{2,1,0:T(8,128)(2,1)}), bf16[4,128,1024]{2,1,0:T(8,128)(2,1)}, u32[]{:S(2)}, u32[]{:S(2)}) async-start(bf16[4,128,1024]{2,1,0:T(8,128)(2,1)} %reduce-scatter.6.cloned.1.call-done), calls=%async_computation.3 | async-start | bytes 2097152 | tf_op jit(solution)/shard_map/all_to_all | solution.py:133
  279.8 2.4 copy-start.2
  279.8 4.4 %copy-start.1 = (bf16[1,64,4096]{2,1,0:T(8,128)(2,1)S(1)}, bf16[1,64,4096]{2,1,0:T(8,128)(2,1)}, u32[]{:S(2)}) copy-start(bf16[1,64,4096]{2,1,0:T(8,128)(2,1)} %param.28) | copy-start | bytes 1572868
Sparse Core Ops, SparseCore 0:
  17.3 46.5 reduce-scatter.3
  66.2 27.2 all-gather.2
  111.1 27.9 all-gather.4
  177.2 75.3 reduce-scatter.5
  254.7 21.9 reduce-scatter.7
where the time goes:
time: 291 us
  waiting for transfers between devices  143 us (49%)
  blocking collectives  50.9 us (17%)
  matrix products  36.6 us (13%)
  local copies, waits for them, and re-layouts  20.7 us (7%)
  other arithmetic  16.2 us (6%)
  between operations  14.1 us (5%)
  starting transfers between devices  9.47 us (3%)
    all_to_all x1, blocking collectives, local(): lax.all_to_all(grad_part, 'route', split_axis=0, concat_axis=0, tiled=True)  50.9 us
    all_to_all x1, waiting for transfers between devices, local(): lax.all_to_all(token_part, 'route', split_axis=0, concat_axis=0, tiled=True)  47.4 us
    reduce_scatter x1, waiting for transfers between devices, local(): lax.psum_scatter(head_terms, 'cuts', scatter_dimension=1, tiled=True)  46.7 us
    all_gather x1, waiting for transfers between devices, local(): lax.all_gather(hidden_cols, 'cuts', axis=1, tiled=True)  25.8 us
    reduce_scatter x1, waiting for transfers between devices, local(): lax.psum_scatter(gradient_pieces.astype(jnp.bfloat16), 'cuts', scatter_di...  18.7 us
    dot_general x1, matrix products, local(): jnp.dot(activ, expert_down_weight[0], preferred_element_type=jnp.float32)  9.11 us
    gather x2, local copies, waits for them, and re-layouts, fill_slots(): return jnp.take(padded, owners, axis=0)  8.77 us
    dot_general x1, matrix products, local(): lax.dot_general(expert_input_rows, expert_gate_weight[0], reduce_final_ax...  7 us
  transfers between devices with their start and end apart: 7, of which 5 were waited for; matrix products, arithmetic and copies ran while one was open for 16% of the time, Pallas kernels for 0%

commit v1 on v0

--- a/solution.py
+++ b/solution.py
@@ -1,8 +1,11 @@
+import functools
 import math
 
 import jax
 import jax.numpy as jnp
 from jax import lax
+from jax.experimental import pallas as pl
+from jax.experimental.pallas import tpu as pltpu
 from jax.sharding import PartitionSpec as P
 
 HEAD_DIM = 128
@@ -51,7 +54,7 @@
     return router_choice_weight[:, 0:1] * first_out + router_choice_weight[:, 1:2] * second_out
 
 
-def local(
+def exchanged_slots(
     query_matrix_rows,
     key_matrix_rows,
     value_matrix_rows,
@@ -164,9 +167,635 @@
     return (layer_out, down_factor_gradient[None], up_factor_gradient[None])
 
 
+MESH = pl.DeviceIdType.MESH
+NT = (((1,), (1,)), ((), ()))
+VMEM_GRANT = 60 * 2**20
+
+
+def fused_kernel(
+    n_r,
+    n_c,
+    q_ref,
+    k_ref,
+    v_ref,
+    res_ref,
+    cot_ref,
+    wt_ref,
+    adn_ref,
+    aup_ref,
+    wo_hbm,
+    gate_hbm,
+    down_hbm,
+    out_ref,
+    dgrad_ref,
+    ugrad_ref,
+    wo,
+    gate,
+    down,
+    xbuf,
+    gbuf,
+    part,
+    rs_in,
+    opart,
+    core_in,
+    y_in,
+    oz_in,
+    acc_p,
+    acc_g,
+    low,
+    act,
+    gpre,
+    att,
+    hid,
+    fac,
+    wbuf,
+    wcol,
+    load_sem,
+    ag_send,
+    ag_recv,
+    rs_send,
+    rs_recv,
+    core_send,
+    core_recv,
+    y_send,
+    y_recv,
+    oz_send,
+    oz_recv,
+    f_send,
+    f_recv,
+    w_send,
+    w_recv,
+):
+    f32 = jnp.float32
+    bf16 = jnp.bfloat16
+    grp = lax.axis_index("group")
+    r = lax.axis_index("route")
+    c = lax.axis_index("cuts")
+    core = r % 2
+    chip = r // 2
+    r_core = chip * 2 + (1 - core)
+    r_y = (1 - chip) * 2 + core
+    r_diag = (1 - chip) * 2 + (1 - core)
+    rows, cols = res_ref.shape
+
+    def rslice(s):
+        return pl.ds(pl.multiple_of(s * rows, rows), rows)
+
+    def cslice(j):
+        return pl.ds(pl.multiple_of(j * cols, cols), cols)
+
+    def remote(src, dst, ss, rs, dr, dc):
+        return pltpu.make_async_remote_copy(
+            src_ref=src,
+            dst_ref=dst,
+            send_sem=ss,
+            recv_sem=rs,
+            device_id=(grp, dr, dc),
+            device_id_type=MESH,
+        )
+
+    barrier = pltpu.get_barrier_semaphore()
+    for d in range(1, n_r):
+        pl.semaphore_signal(
+            barrier, inc=1, device_id=(grp, (r + d) % n_r, c), device_id_type=MESH
+        )
+    for d in range(1, n_c):
+        pl.semaphore_signal(
+            barrier, inc=1, device_id=(grp, r, (c + d) % n_c), device_id_type=MESH
+        )
+
+    def slot_of(t):
+        k = n_c - 1 - t // 2
+        j = jnp.where(t % 2 == 0, c + k, c - k)
+        return k, j, (j >= 0) & (j < n_c) & ((k > 0) | (t % 2 == 0))
+
+    n_slots = 2 * n_c - 1
+
+    def wo_copy(j):
+        return pltpu.make_async_copy(
+            wo_hbm.at[:, cslice(j)], wo.at[:, cslice(j)], load_sem.at[j]
+        )
+
+    def each_slot(body):
+        def step(t, carry):
+            k, j, ok = slot_of(t)
+
+            @pl.when(ok)
+            def _():
+                body(k, j)
+
+            return carry
+
+        lax.fori_loop(0, n_slots, step, 0)
+
+    each_slot(lambda k, j: wo_copy(j).start())
+    down_copy = pltpu.make_async_copy(down_hbm, down, load_sem.at[n_c])
+    gate_copy = pltpu.make_async_copy(gate_hbm, gate, load_sem.at[n_c + 1])
+    down_copy.start()
+    gate_copy.start()
+
+    gbuf[c, rslice(r)] = cot_ref[...]
+    wbuf[r] = wt_ref[...]
+    pl.semaphore_wait(barrier, n_r - 1 + n_c - 1)
+
+    def ag(kind, buf, what, j, s, dr, dc):
+        place = buf.at[j, rslice(s)]
+        return remote(
+            place, place, ag_send.at[kind, what, j], ag_recv.at[kind, j, s], dr, dc
+        )
+
+    def up(kind, buf, j):
+        return ag(kind, buf, 0, j, r, r, jnp.minimum(c + 1, n_c - 1))
+
+    def dn(kind, buf, j):
+        return ag(kind, buf, 1, j, r, r, jnp.maximum(c - 1, 0))
+
+    def across(kind, buf, j):
+        return ag(kind, buf, 2, j, r, r_y, c)
+
+    def own_core(kind, buf, j):
+        return ag(kind, buf, 3, j, r, r_core, c)
+
+    def fwd_core(kind, buf, j):
+        return ag(kind, buf, 4, j, r_y, r_core, c)
+
+    def arrived(kind, buf, j, s):
+        ag(kind, buf, 0, j, s, r_core, c).wait_recv()
+
+    def spread(kind, buf, j):
+        across(kind, buf, j).start()
+
+        @pl.when((j <= c) & (c < n_c - 1))
+        def _():
+            up(kind, buf, j).start()
+
+        @pl.when((j >= c) & (c > 0))
+        def _():
+            dn(kind, buf, j).start()
+
+        own_core(kind, buf, j).start()
+
+    def both_sides(k, body):
+        @pl.when(c - k >= 0)
+        def _():
+            body(c - k)
+
+        @pl.when((c + k < n_c) & (k > 0))
+        def _():
+            body(c + k)
+
+    def z_stage(kind, buf, k):
+        def one(j):
+            arrived(kind, buf, j, r)
+            spread(kind, buf, j)
+
+        both_sides(k, one)
+
+    def y_stage(kind, buf, k):
+        def one(j):
+            arrived(kind, buf, j, r_y)
+            fwd_core(kind, buf, j).start()
+
+        both_sides(k, one)
+
+    def c_stage(kind, buf, k, body):
+        def step(side, carry):
+            j = jnp.where(side == 0, c - k, c + k)
+
+            @pl.when((j >= 0) & (j < n_c) & ((k > 0) | (side == 0)))
+            def _():
+                arrived(kind, buf, j, r_core)
+                arrived(kind, buf, j, r_diag)
+                body(j)
+
+            return carry
+
+        lax.fori_loop(0, 2, step, 0)
+
+    def ag_finish(kind, buf):
+        def step(j, carry):
+            across(kind, buf, j).wait_send()
+
+            @pl.when((j <= c) & (c < n_c - 1))
+            def _():
+                up(kind, buf, j).wait_send()
+
+            @pl.when((j >= c) & (c > 0))
+            def _():
+                dn(kind, buf, j).wait_send()
+
+            own_core(kind, buf, j).wait_send()
+            fwd_core(kind, buf, j).wait_send()
+            return carry
+
+        lax.fori_loop(0, n_c, step, 0)
+
+    spread(0, gbuf, c)
+
+    def w_copy(d):
+        return remote(
+            wbuf.at[r], wbuf.at[r], w_send.at[d], w_recv.at[r], (r + d) % n_r, c
+        )
+
+    for d in range(1, n_r):
+        w_copy(d).start()
+
+    kv_heads = k_ref.shape[1] // HEAD_DIM
+    heads = q_ref.shape[1] // HEAD_DIM
+    future = lax.broadcasted_iota(jnp.int32, (rows, rows), 1) > lax.broadcasted_iota(
+        jnp.int32, (rows, rows), 0
+    )
+    for h in range(heads):
+        g = h // (heads // kv_heads)
+        sc = lax.dot_general(
+            q_ref[:, h * HEAD_DIM : (h + 1) * HEAD_DIM],
+            k_ref[:, g * HEAD_DIM : (g + 1) * HEAD_DIM],
+            NT,
+            preferred_element_type=f32,
+        ) / math.sqrt(HEAD_DIM)
+        sc = jnp.where(future, -jnp.inf, sc)
+        ex = jnp.exp(sc - jnp.max(sc, axis=-1, keepdims=True))
+        wts = (ex / jnp.sum(ex, axis=-1, keepdims=True)).astype(bf16)
+        att[:, h * HEAD_DIM : (h + 1) * HEAD_DIM] = jnp.dot(
+            wts,
+            v_ref[:, g * HEAD_DIM : (g + 1) * HEAD_DIM],
+            preferred_element_type=f32,
+        ).astype(bf16)
+
+    def line_copy(buf_at, inbox, ss, rs, j, upward):
+        dc = jnp.minimum(c + 1, n_c - 1) if upward else jnp.maximum(c - 1, 0)
+        side = 0 if upward else 1
+        return remote(buf_at(j), inbox.at[side, j], ss.at[j], rs.at[side, j], r, dc)
+
+    def line_step(buf_at, load, store, inbox, ss, rs, j):
+        @pl.when(j > c)
+        def _():
+            @pl.when(c > 0)
+            def _():
+                line_copy(buf_at, inbox, ss, rs, j, True).wait_recv()
+                store(j, load(j) + inbox[0, j].astype(f32))
+
+            line_copy(buf_at, inbox, ss, rs, j, True).start()
+
+        @pl.when(j < c)
+        def _():
+            @pl.when(c < n_c - 1)
+            def _():
+                line_copy(buf_at, inbox, ss, rs, j, False).wait_recv()
+                store(j, load(j) + inbox[1, j].astype(f32))
+
+            line_copy(buf_at, inbox, ss, rs, j, False).start()
+
+    def line_final(buf_at, inbox, ss, rs, total):
+        @pl.when(c > 0)
+        def _():
+            line_copy(buf_at, inbox, ss, rs, c, True).wait_recv()
+            total[...] += inbox[0, c].astype(f32)
+
+        @pl.when(c < n_c - 1)
+        def _():
+            line_copy(buf_at, inbox, ss, rs, c, False).wait_recv()
+            total[...] += inbox[1, c].astype(f32)
+
+    def line_finish(buf_at, inbox, ss, rs):
+        def step(j, carry):
+            @pl.when(j != c)
+            def _():
+                line_copy(buf_at, inbox, ss, rs, j, True).wait_send()
+
+            return carry
+
+        lax.fori_loop(0, n_c, step, 0)
+
+    def part_at(j):
+        return part.at[j]
+
+    def part_load(j):
+        return part[j].astype(f32)
+
+    def part_store(j, value):
+        part[j] = value.astype(bf16)
+
+    def project(j):
+        wo_copy(j).wait()
+        return jnp.dot(att[...], wo[:, cslice(j)], preferred_element_type=f32)
+
+    def rs_loop(i, carry):
+        k = n_c - 1 - i
+
+        def side_step(side, carry2):
+            j = jnp.where(side == 0, c + k, c - k)
+
+            @pl.when((j >= 0) & (j < n_c))
+            def _():
+                part[j] = project(j).astype(bf16)
+                line_step(part_at, part_load, part_store, rs_in, rs_send, rs_recv, j)
+
+            return carry2
+
+        lax.fori_loop(0, 2, side_step, 0)
+        z_stage(0, gbuf, i + 1)
+        y_stage(0, gbuf, i)
+        return carry
+
+    lax.fori_loop(0, n_c - 1, rs_loop, 0)
+    hid[...] = res_ref[...].astype(f32) + project(c)
+    line_final(part_at, rs_in, rs_send, rs_recv, hid)
+    xbuf[c, rslice(r)] = hid[...].astype(bf16)
+    spread(1, xbuf, c)
+    y_stage(0, gbuf, n_c - 1)
+
+    acc_p[...] = jnp.zeros_like(acc_p)
+    acc_g[...] = jnp.zeros_like(acc_g)
+    low[...] = jnp.zeros_like(low)
+    half = 2 * rows
+    n_half = n_r // 2
+
+    def grad_mm(j):
+        def step(m, carry):
+            at = pl.ds(pl.multiple_of(m * half, half), half)
+            acc_g[at] += lax.dot_general(
+                gbuf[j, at], down[:, cslice(j)], NT, preferred_element_type=f32
+            )
+            return carry
+
+        lax.fori_loop(0, n_half, step, 0)
+
+    def gate_mm(j):
+        def step(m, carry):
+            at = pl.ds(pl.multiple_of(m * half, half), half)
+            x = xbuf[j, at]
+            acc_p[at] += lax.dot_general(
+                x, gate[:, cslice(j)], NT, preferred_element_type=f32
+            )
+            low[at] += lax.dot_general(
+                x, adn_ref[:, cslice(j)], NT, preferred_element_type=f32
+            )
+            return carry
+
+        lax.fori_loop(0, n_half, step, 0)
+
+    down_copy.wait()
+    gate_copy.wait()
+
+    def hidden_loop(i, carry):
+        @pl.when(i <= n_c - 2)
+        def _():
+            z_stage(1, xbuf, i + 1)
+
+        @pl.when(i <= n_c - 1)
+        def _():
+            c_stage(0, gbuf, i, grad_mm)
+            y_stage(1, xbuf, i)
+
+        @pl.when(i >= 1)
+        def _():
+            c_stage(1, xbuf, i - 1, gate_mm)
+
+        return carry
+
+    lax.fori_loop(0, n_c + 1, hidden_loop, 0)
+
+    for d in range(1, n_r):
+        src = (r + d) % n_r
+        remote(
+            wbuf.at[src], wbuf.at[src], w_send.at[d], w_recv.at[src], src, c
+        ).wait_recv()
+
+    eye = lax.broadcasted_iota(jnp.int32, (rows, rows), 1) == lax.broadcasted_iota(
+        jnp.int32, (rows, rows), 0
+    )
+    mine = lax.broadcasted_iota(jnp.int32, wt_ref.shape, 0) == r
+
+    def act_step(i, carry):
+        s = (1 - chip) * 2 + i
+        s = jnp.where(s >= n_r, s - n_r, s)
+        at = rslice(s)
+        w_row = jnp.sum(jnp.where(mine, wbuf[s], 0.0), axis=0, keepdims=True)
+        w = jnp.sum(jnp.where(eye, w_row, 0.0), axis=1, keepdims=True)
+        wcol[at] = jnp.broadcast_to(w, (rows, wcol.shape[1]))
+        z = acc_p[at] + ADAPTER_SCALE * jnp.dot(
+            low[at].astype(bf16), aup_ref[...], preferred_element_type=f32
+        )
+        sig = 1.0 / (1.0 + jnp.exp(-z))
+        act[at] = (z * sig).astype(bf16)
+        gpre[at] = (acc_g[at] * w * (sig * (1.0 + z * (1.0 - sig)))).astype(bf16)
+        return carry
+
+    lax.fori_loop(0, n_r, act_step, 0)
+
+    def out_mm(j, base):
+        at = pl.ds(pl.multiple_of(base * rows, rows), half)
+        prod = jnp.dot(act[at], down[:, cslice(j)], preferred_element_type=f32)
+        opart[j, at] = (prod * wcol[at, 0:1]).astype(bf16)
+
+    def core_copy(which, j, s):
+        return remote(
+            opart.at[j, rslice(s)],
+            core_in.at[which, j],
+            core_send.at[which, j],
+            core_recv.at[which, j],
+            r_core,
+            c,
+        )
+
+    def y_copy(j):
+        return remote(
+            opart.at[j, rslice(r_y)], y_in.at[j], y_send.at[j], y_recv.at[j], r_y, c
+        )
+
+    def other_mm(k, j):
+        out_mm(j, (1 - chip) * 2)
+        core_copy(0, j, r_diag).start()
+
+    def other_pair(k, j):
+        core_copy(0, j, r_diag).wait_recv()
+        at = rslice(r_y)
+        opart[j, at] = (opart[j, at].astype(f32) + core_in[0, j].astype(f32)).astype(bf16)
+        y_copy(j).start()
+
+    def other_loop(t, carry):
+        k, j, ok = slot_of(t)
+
+        @pl.when(ok & (t < n_slots))
+        def _():
+            other_mm(k, j)
+
+        k1, j1, ok1 = slot_of(t - 1)
+
+        @pl.when(ok1 & (t > 0))
+        def _():
+            other_pair(k1, j1)
+
+        return carry
+
+    lax.fori_loop(0, n_slots + 1, other_loop, 0)
+
+    fac[c] = lax.dot_general(
+        aup_ref[...], gpre[...], NT, preferred_element_type=f32
+    ).astype(bf16)
+
+    def f_copy(d, owner):
+        return remote(
+            fac.at[owner], fac.at[owner], f_send.at[d], f_recv.at[owner], r, (c + d) % n_c
+        )
+
+    for d in range(1, n_c):
+        f_copy(d, c).start()
+
+    def own_mm(k, j):
+        out_mm(j, chip * 2)
+        core_copy(1, j, r_core).start()
+
+    each_slot(own_mm)
+
+    ugrad_ref[...] = ADAPTER_SCALE * jnp.dot(
+        low[...].T.astype(bf16), gpre[...], preferred_element_type=f32
+    )
+    for d in range(1, n_c):
+        f_copy(d, (c + d) % n_c).wait_recv()
+    total_f = fac[0].astype(f32)
+    for d in range(1, n_c):
+        total_f = total_f + fac[d].astype(f32)
+    dgrad_ref[...] = ADAPTER_SCALE * jnp.dot(
+        total_f.astype(bf16), xbuf[c], preferred_element_type=f32
+    )
+
+    def out_at(j):
+        return opart.at[j, rslice(r)]
+
+    def out_load(j):
+        return opart[j, rslice(r)].astype(f32)
+
+    def out_store(j, value):
+        opart[j, rslice(r)] = value.astype(bf16)
+
+    def route_total(j):
+        core_copy(1, j, r_core).wait_recv()
+        y_copy(j).wait_recv()
+        return out_load(j) + core_in[1, j].astype(f32) + y_in[j].astype(f32)
+
+    def reduce_step(k, j):
+        @pl.when(k > 0)
+        def _():
+            out_store(j, route_total(j))
+            line_step(out_at, out_load, out_store, oz_in, oz_send, oz_recv, j)
+
+    each_slot(reduce_step)
+    hid[...] = xbuf[c, rslice(r)].astype(f32) + route_total(c)
+    line_final(out_at, oz_in, oz_send, oz_recv, hid)
+    out_ref[...] = hid[...].astype(bf16)
+
+    ag_finish(0, gbuf)
+    ag_finish(1, xbuf)
+    line_finish(part_at, rs_in, rs_send, rs_recv)
+    line_finish(out_at, oz_in, oz_send, oz_recv)
+    for d in range(1, n_r):
+        w_copy(d).wait_send()
+    for d in range(1, n_c):
+        f_copy(d, c).wait_send()
+
+    def last(j, carry):
+        core_copy(0, j, r_diag).wait_send()
+        core_copy(1, j, r_core).wait_send()
+        y_copy(j).wait_send()
+        return carry
+
+    lax.fori_loop(0, n_c, last, 0)
+
+
+def scratch_list(n_r, n_c, rows, cols, inner, units, rank, w_rows):
+    bf16 = jnp.bfloat16
+    f32 = jnp.float32
+    dma = pltpu.SemaphoreType.DMA
+    width = n_c * cols
+    tokens = n_r * rows
+    return [
+        pltpu.VMEM((inner, width), bf16),
+        pltpu.VMEM((units, width), bf16),
+        pltpu.VMEM((units, width), bf16),
+        pltpu.VMEM((n_c, tokens, cols), bf16),
+        pltpu.VMEM((n_c, tokens, cols), bf16),
+        pltpu.VMEM((n_c, rows, cols), bf16),
+        pltpu.VMEM((2, n_c, rows, cols), bf16),
+        pltpu.VMEM((n_c, tokens, cols), bf16),
+        pltpu.VMEM((2, n_c, rows, cols), bf16),
+        pltpu.VMEM((n_c, rows, cols), bf16),
+        pltpu.VMEM((2, n_c, rows, cols), bf16),
+        pltpu.VMEM((tokens, units), f32),
+        pltpu.VMEM((tokens, units), f32),
+        pltpu.VMEM((tokens, rank), f32),
+        pltpu.VMEM((tokens, units), bf16),
+        pltpu.VMEM((tokens, units), bf16),
+        pltpu.VMEM((rows, inner), bf16),
+        pltpu.VMEM((rows, cols), f32),
+        pltpu.VMEM((n_c, rank, tokens), bf16),
+        pltpu.VMEM((n_r, w_rows, rows), f32),
+        pltpu.VMEM((tokens, 128), f32),
+        dma((n_c + 2,)),
+        dma((2, 5, n_c)),
+        dma((2, n_c, n_r)),
+        dma((n_c,)),
+        dma((2, n_c)),
+        dma((2, n_c)),
+        dma((2, n_c)),
+        dma((n_c,)),
+        dma((n_c,)),
+        dma((n_c,)),
+        dma((2, n_c)),
+        dma((n_c,)),
+        dma((n_c,)),
+        dma((n_r,)),
+        dma((n_r,)),
+    ]
+
+
+def dense_tokens(n_r, n_c, *args):
+    (q, k, v, wo, res, cot, choices, _, router, gate, down, adn, aup) = args
+    rows, cols = res.shape
+    units = gate.shape[1]
+    rank = adn.shape[1]
+    w_rows = -(-n_r // 8) * 8
+    hits = choices.T[:, None, :] == jnp.arange(w_rows, dtype=jnp.int32)[None, :, None]
+    wt = jnp.sum(jnp.where(hits, router.T[:, None, :], 0.0), axis=0)
+    vmem = pl.BlockSpec(memory_space=pltpu.VMEM)
+    hbm = pl.BlockSpec(memory_space=pltpu.HBM)
+    tokens = n_r * rows
+    outs = pl.pallas_call(
+        functools.partial(fused_kernel, n_r, n_c),
+        out_shape=(
+            jax.ShapeDtypeStruct((rows, cols), jnp.bfloat16),
+            jax.ShapeDtypeStruct((rank, cols), jnp.float32),
+            jax.ShapeDtypeStruct((rank, units), jnp.float32),
+        ),
+        in_specs=[vmem] * 8 + [hbm] * 3,
+        out_specs=(vmem, vmem, vmem),
+        scratch_shapes=scratch_list(
+            n_r, n_c, rows, cols, q.shape[1], units, rank, w_rows
+        ),
+        compiler_params=pltpu.CompilerParams(
+            collective_id=0, has_side_effects=True, vmem_limit_bytes=VMEM_GRANT
+        ),
+        cost_estimate=pl.CostEstimate(
+            flops=6 * tokens * units * cols * n_c,
+            bytes_accessed=2 * (q.shape[1] + 2 * units) * cols * n_c,
+            transcendentals=tokens * units,
+        ),
+    )(q, k, v, res, cot, wt, adn[0], aup[0], wo, gate[0], down[0])
+    return outs[0], outs[1][None], outs[2][None]
+
+
+def local(n_r, n_c, *args):
+    length = args[4].shape[0]
+    capacity = 4 * length // n_r
+    if capacity == length and n_r == 2 * 2:
+        return dense_tokens(n_r, n_c, *args)
+    return exchanged_slots(*args)
+
+
 def solution(mesh):
     return jax.shard_map(
-        local,
+        functools.partial(local, mesh.shape["route"], mesh.shape["cuts"]),
         mesh=mesh,
         in_specs=(
             P(("group", "route"), "cuts"),

time: 291 us -> 114 us (0.39)
  waiting for transfers between devices: 143 us -> 0 us
  Pallas kernels: 0 us -> 107 us
  blocking collectives: 50.9 us -> 0 us
  matrix products: 36.6 us -> 0 us
  local copies, waits for them, and re-layouts: 20.7 us -> 4.98 us
  other arithmetic: 16.2 us -> 1.29 us
  between operations: 14.1 us -> 0.64 us
  starting transfers between devices: 9.47 us -> 0 us
    pallas_call x0 -> x1, Pallas kernels: none -> 107 us  [dense_tokens(): pl.pallas_call(functools.partial(fused_kernel, n_r, n_c), out_shape=(jax....]
    reduce_scatter x3 -> x0, waiting for transfers between devices: 68.7 us -> none  [the longest x1 46.7 us: local(): lax.psum_scatter(head_terms, 'cuts', scatter_dimension=1, tiled=True)]
    all_to_all x1 -> x0, blocking collectives: 50.9 us -> none  [local(): lax.all_to_all(grad_part, 'route', split_axis=0, concat_axis=0, tiled=True)]
    all_to_all x2 -> x0, waiting for transfers between devices: 47.4 us -> none  [the longest x1 47.4 us: local(): lax.all_to_all(token_part, 'route', split_axis=0, concat_axis=0, tiled=True)]
    dot_general x10 -> x0, matrix products: 36.3 us -> none  [the longest x1 9.11 us: local(): jnp.dot(activ, expert_down_weight[0], preferred_element_type=jnp.float32)]
    all_gather x2 -> x0, waiting for transfers between devices: 25.8 us -> none  [the longest x1 25.8 us: local(): lax.all_gather(hidden_cols, 'cuts', axis=1, tiled=True)]
    gather x4 -> x0, local copies, waits for them, and re-layouts: 11.2 us -> none  [the longest x2 8.77 us: fill_slots(): return jnp.take(padded, owners, axis=0)]
    all_to_all x2 -> x0, starting transfers between devices: 9.09 us -> none  [the longest x1 4.84 us: local(): lax.all_to_all(token_part, 'route', split_axis=0, concat_axis=0, tiled=True)]
  transfers between devices with their start and end apart: 7 -> 0, of which waited for: 5 -> 0; matrix products, arithmetic and copies ran while one was open for 16% -> 0% of each run, Pallas kernels for 0% -> 0%
where the time goes in v1:
time: 114 us
  Pallas kernels  107 us (94%)
  local copies, waits for them, and re-layouts  4.98 us (4%)
  other arithmetic  1.29 us (1%)
    pallas_call x1, Pallas kernels, dense_tokens(): pl.pallas_call(functools.partial(fused_kernel, n_r, n_c), out_shape=(jax....  107 us
    unnamed x3, local copies, waits for them, and re-layouts  4.98 us

profile of v1, /device:TPU:0, one launch (start us, length us, event | category | flops | bytes accessed | tf_op | source)
XLA Modules:
  0.0 114.0 jit_solution(4972837530055243117)
XLA Ops:
  0.6 1.3 %select_reduce_fusion.wt_ref = f32[8,128]{1,0:T(8,128)} fusion(f32[2,128]{1,0:T(2,128)} %bitcast.10, s32[2,128]{1,0:T(2,128)} %bitcast.11), kind=kLoop, calls=%fused_computation | loop fusion | flops 5120 | bytes 6144 | tf_op jit(solution)/shard_map/reduce_sum | solution.py:760
  1.9 107.1 %shard_map.139 = (bf16[128,1024]{1,0:T(8,128)(2,1)}, f32[64,1024]{1,0:T(8,128)}, f32[64,800]{1,0:T(8,128)}) custom-call(bf16[128,1024]{1,0:T(8,128)(2,1)} %q_ref.1, bf16[128,256]{1,0:T(8,128)(2,1)} %k_ref.1, bf16[128,256]{1,0:T(8,128)(2,1)} %v_ref.1, bf16[128,1024]{1,0:T(8,128)(2,1)} %res_ref.1, bf16[128,1024]{1,0:T(8,128)(2,1)} %cot_ref.1, ...), custom_call_target="tpu_custom_call" | custom-call | flops 10066329600 | bytes 21495808 | tf_op jit(solution)/shard_map/pallas_call | solution.py:764
  109.0 1.7 %copy.18 = bf16[128,1024]{1,0:T(8,128)(2,1)} copy(bf16[128,1024]{1,0:T(8,128)(2,1)} %get-tuple-element.12) | data formatting | bytes 524288
  110.7 1.7 %copy.19 = f32[1,64,1024]{2,1,0:T(8,128)} copy(f32[1,64,1024]{2,1,0:T(8,128)} %bitcast.8) | data formatting | bytes 524288
  112.4 1.6 %copy.20 = f32[1,64,800]{2,1,0:T(8,128)} copy(f32[1,64,800]{2,1,0:T(8,128)} %bitcast.9) | data formatting | bytes 409600

commit v2 on v1

--- a/solution.py
+++ b/solution.py
@@ -170,6 +170,7 @@
 MESH = pl.DeviceIdType.MESH
 NT = (((1,), (1,)), ((), ()))
 VMEM_GRANT = 60 * 2**20
+AHEAD = 1
 
 
 def fused_kernel(
@@ -435,6 +436,10 @@
                 line_copy(buf_at, inbox, ss, rs, j, True).wait_recv()
                 store(j, load(j) + inbox[0, j].astype(f32))
 
+            @pl.when(j < n_c - 1)
+            def _():
+                line_copy(buf_at, inbox, ss, rs, j + 1, True).wait_send()
+
             line_copy(buf_at, inbox, ss, rs, j, True).start()
 
         @pl.when(j < c)
@@ -444,6 +449,10 @@
                 line_copy(buf_at, inbox, ss, rs, j, False).wait_recv()
                 store(j, load(j) + inbox[1, j].astype(f32))
 
+            @pl.when(j > 0)
+            def _():
+                line_copy(buf_at, inbox, ss, rs, j - 1, False).wait_send()
+
             line_copy(buf_at, inbox, ss, rs, j, False).start()
 
     def line_final(buf_at, inbox, ss, rs, total):
@@ -458,14 +467,13 @@
             total[...] += inbox[1, c].astype(f32)
 
     def line_finish(buf_at, inbox, ss, rs):
-        def step(j, carry):
-            @pl.when(j != c)
-            def _():
-                line_copy(buf_at, inbox, ss, rs, j, True).wait_send()
-
-            return carry
-
-        lax.fori_loop(0, n_c, step, 0)
+        @pl.when(c < n_c - 1)
+        def _():
+            line_copy(buf_at, inbox, ss, rs, c + 1, True).wait_send()
+
+        @pl.when(c > 0)
+        def _():
+            line_copy(buf_at, inbox, ss, rs, c - 1, False).wait_send()
 
     def part_at(j):
         return part.at[j]
@@ -495,7 +503,6 @@
 
         lax.fori_loop(0, 2, side_step, 0)
         z_stage(0, gbuf, i + 1)
-        y_stage(0, gbuf, i)
         return carry
 
     lax.fori_loop(0, n_c - 1, rs_loop, 0)
@@ -503,7 +510,7 @@
     line_final(part_at, rs_in, rs_send, rs_recv, hid)
     xbuf[c, rslice(r)] = hid[...].astype(bf16)
     spread(1, xbuf, c)
-    y_stage(0, gbuf, n_c - 1)
+    lax.fori_loop(0, n_c, lambda i, z: (y_stage(0, gbuf, i), z)[1], 0)
 
     acc_p[...] = jnp.zeros_like(acc_p)
     acc_g[...] = jnp.zeros_like(acc_g)
@@ -608,28 +615,26 @@
         out_mm(j, (1 - chip) * 2)
         core_copy(0, j, r_diag).start()
 
-    def other_pair(k, j):
+    def far(i):
+        below = jnp.minimum(c, n_c - 1 - c)
+        single = n_c - 1 - 2 * below
+        d = n_c - 1 - below - i
+        one_side = jnp.where(c < n_c - 1 - c, c + d, c - d)
+        e = i - single
+        kk = below - e // 2
+        two_side = jnp.where(e % 2 == 0, c + kk, c - kk)
+        return jnp.where(i >= single, two_side, one_side)
+
+    def other_pair(i):
+        j = far(i)
         core_copy(0, j, r_diag).wait_recv()
         at = rslice(r_y)
         opart[j, at] = (opart[j, at].astype(f32) + core_in[0, j].astype(f32)).astype(bf16)
         y_copy(j).start()
 
-    def other_loop(t, carry):
-        k, j, ok = slot_of(t)
-
-        @pl.when(ok & (t < n_slots))
-        def _():
-            other_mm(k, j)
-
-        k1, j1, ok1 = slot_of(t - 1)
-
-        @pl.when(ok1 & (t > 0))
-        def _():
-            other_pair(k1, j1)
-
-        return carry
-
-    lax.fori_loop(0, n_slots + 1, other_loop, 0)
+    each_slot(other_mm)
+    for i in range(AHEAD):
+        other_pair(i)
 
     fac[c] = lax.dot_general(
         aup_ref[...], gpre[...], NT, preferred_element_type=f32
@@ -675,13 +680,17 @@
         y_copy(j).wait_recv()
         return out_load(j) + core_in[1, j].astype(f32) + y_in[j].astype(f32)
 
-    def reduce_step(k, j):
-        @pl.when(k > 0)
-        def _():
-            out_store(j, route_total(j))
-            line_step(out_at, out_load, out_store, oz_in, oz_send, oz_recv, j)
-
-    each_slot(reduce_step)
+    def reduce_loop(i, carry):
+        j = far(i)
+        out_store(j, route_total(j))
+        @pl.when(i + AHEAD < n_c)
+        def _():
+            other_pair(i + AHEAD)
+
+        line_step(out_at, out_load, out_store, oz_in, oz_send, oz_recv, j)
+        return carry
+
+    lax.fori_loop(0, n_c - 1, reduce_loop, 0)
     hid[...] = xbuf[c, rslice(r)].astype(f32) + route_total(c)
     line_final(out_at, oz_in, oz_send, oz_recv, hid)
     out_ref[...] = hid[...].astype(bf16)
@@ -750,6 +759,11 @@
     ]
 
 
+def settle(*refs):
+    for src, dst in zip(refs[:3], refs[3:]):
+        dst[...] = src[...]
+
+
 def dense_tokens(n_r, n_c, *args):
     (q, k, v, wo, res, cot, choices, _, router, gate, down, adn, aup) = args
     rows, cols = res.shape
@@ -782,6 +796,12 @@
             transcendentals=tokens * units,
         ),
     )(q, k, v, res, cot, wt, adn[0], aup[0], wo, gate[0], down[0])
+    outs = pl.pallas_call(
+        settle,
+        out_shape=[jax.ShapeDtypeStruct(o.shape, o.dtype) for o in outs],
+        in_specs=[vmem] * 3,
+        out_specs=[vmem] * 3,
+    )(*outs)
     return outs[0], outs[1][None], outs[2][None]
 
 

time: 114 us -> 99.4 us (0.87)
  Pallas kernels: 107 us -> 97.3 us
  local copies, waits for them, and re-layouts: 4.98 us -> 0 us
    pallas_call x1, Pallas kernels: 107 us -> 95.3 us  [dense_tokens(): pl.pallas_call(functools.partial(fused_kernel, n_r, n_c), out_shape=(jax....]
    unnamed x3 -> x0, local copies, waits for them, and re-layouts: 4.98 us -> none
    pallas_call x0 -> x1, Pallas kernels: none -> 1.98 us  [dense_tokens(): pl.pallas_call(settle, out_shape=[jax.ShapeDtypeStruct(o.shape, o.dtype)...]
where the time goes in v2:
time: 99.4 us; the launch traced here: 99.2 us
  Pallas kernels  97.3 us (98%)
  other arithmetic  1.29 us (1%)
    pallas_call x1, Pallas kernels, dense_tokens(): pl.pallas_call(functools.partial(fused_kernel, n_r, n_c), out_shape=(jax....  95.3 us

profile of v2, /device:TPU:0, one launch (start us, length us, event | category | flops | bytes accessed | tf_op | source)
XLA Modules:
  0.0 99.2 jit_solution(8210445229047386016)
XLA Ops:
  0.6 1.3 %select_reduce_fusion.wt_ref = f32[8,128]{1,0:T(8,128)} fusion(f32[2,128]{1,0:T(2,128)} %bitcast.8, s32[2,128]{1,0:T(2,128)} %bitcast.9), kind=kLoop, calls=%fused_computation | loop fusion | flops 5120 | bytes 6144 | tf_op jit(solution)/shard_map/reduce_sum | solution.py:774
  1.9 95.3 %shard_map.139 = (bf16[128,1024]{1,0:T(8,128)(2,1)}, f32[64,1024]{1,0:T(8,128)}, f32[64,800]{1,0:T(8,128)}) custom-call(bf16[128,1024]{1,0:T(8,128)(2,1)} %q_ref.1, bf16[128,256]{1,0:T(8,128)(2,1)} %k_ref.1, bf16[128,256]{1,0:T(8,128)(2,1)} %v_ref.1, bf16[128,1024]{1,0:T(8,128)(2,1)} %res_ref.1, bf16[128,1024]{1,0:T(8,128)(2,1)} %cot_ref.1, ...), custom_call_target="tpu_custom_call" | custom-call | flops 10066329600 | bytes 21495808 | tf_op jit(solution)/shard_map/pallas_call | solution.py:778
  97.3 2.0 %shard_map.140 = (bf16[128,1024]{1,0:T(8,128)(2,1)}, f32[64,1024]{1,0:T(8,128)}, f32[64,800]{1,0:T(8,128)}) custom-call(bf16[128,1024]{1,0:T(8,128)(2,1)} %get-tuple-element.9.refs_0_, f32[64,1024]{1,0:T(8,128)} %get-tuple-element.10.refs_1_, f32[64,800]{1,0:T(8,128)} %get-tuple-element.11.refs_2_), custom_call_target="tpu_custom_call" | custom-call | tf_op jit(solution)/shard_map/pallas_call | solution.py:799
